TPU v7x, 128 devices: a whole 4x4x4 slice. The times are simulated.
128 devices in a mesh: tm: 8 (over z, y_lo), rowblk: 4 (over y_hi, core), colblk: 4 (over x).
Axes of the slice: x: 4, y: 4 (y_hi: 2, y_lo: 2; y = y_hi * 2 + y_lo), z: 4, core: 2. Of those that a mesh axis runs over, the one named last changes fastest.
Arguments:
- signal: bfloat16 [6144, 16384], P('tm', ('rowblk', 'colblk')), may hold values from -180 to 180
- tile_owner: int32 [128], replicated, may hold values from 0 to 15, as said below
Outputs:
- covariance: float32 [16, 16, 8, 128, 512], P(('rowblk', 'colblk'), 'tm')
Inputs may be any that keep to these rules, and one draw needn't show every extreme that they name: `tile_owner`: each channel block's tiles go to distinct owners (at most one tile of a block to one owner); every owner has between 4 and 16 first tiles, and some owner exactly 16.
All inputs are finite; a program needn't handle non-finite values.
Results may differ from a plain program's by a relative error of at most 0.015.
Values may be sent and summed in bfloat16 or wider, within the bound.
A program may use at most 128 MiB of HBM per device.

v0:
```python
import jax
import jax.numpy as jnp
from jax import lax
from jax.sharding import PartitionSpec as P

TILE = 128
LAGS = 8
APER = 3
OCAP = 16


def passed_along(block, axis, distance):
    devices = range(lax.axis_size(axis))
    route = [(i - distance, i) for i in devices if i - distance in devices]
    return lax.ppermute(block, axis, route)


def segment_terms(slot_block, seg_rows):
    first_tile = slot_block[:, :seg_rows, :TILE]
    lag_terms = []
    for lag_step in range(LAGS):
        second = slot_block[:, lag_step : lag_step + seg_rows, :]
        lag_terms.append(
            jnp.einsum("kti,ktc->kic", first_tile, second, preferred_element_type=jnp.float32)
        )
    return jnp.stack(lag_terms, axis=1)


def route_windows(outgoing):
    incoming = lax.all_to_all(
        outgoing, ("rowblk", "colblk"), split_axis=0, concat_axis=0, tiled=True
    )
    return incoming


def shards(signal, tile_owner):
    seg_rows, local_width = signal.shape
    tiles_here = local_width // TILE
    owners = lax.axis_size(("rowblk", "colblk"))
    segments = lax.axis_size("tm")
    total_time = seg_rows * segments
    win_width = (APER + 1) * TILE
    values = signal.astype(jnp.float32)
    power_sum = lax.psum(jnp.sum(values * values, axis=0), "tm")
    normed = (values * lax.rsqrt(power_sum / total_time + 1e-06)).astype(jnp.bfloat16)
    following = passed_along(normed[:, : APER * TILE], ("rowblk", "colblk"), -1)
    extended = jnp.concatenate([normed, following], axis=1)
    later_rows = passed_along(extended[: LAGS - 1], "tm", -1)
    extended = jnp.concatenate([extended, later_rows], axis=0)
    my_index = lax.axis_index(("rowblk", "colblk"))
    owner_table = tile_owner.reshape(owners, tiles_here)
    my_owners = lax.dynamic_index_in_dim(owner_table, my_index, 0, keepdims=False)
    targets = jnp.arange(owners, dtype=jnp.int32)
    matches = my_owners[None, :] == targets[:, None]
    local_pos = jnp.sum(
        jnp.where(matches, jnp.arange(tiles_here, dtype=jnp.int32)[None, :], 0), axis=1
    )
    present = jnp.any(matches, axis=1)
    arrived = jnp.any(owner_table == my_index, axis=1)
    slot_rank = jnp.cumsum(arrived.astype(jnp.int32)) - 1
    picker = (slot_rank[None, :] == jnp.arange(OCAP, dtype=jnp.int32)[:, None]) & arrived[None, :]
    source_of = jnp.sum(jnp.where(picker, targets[None, :], 0), axis=1)
    filled = jnp.any(picker, axis=1)

    def cut_window(tile_pos):
        return lax.dynamic_slice_in_dim(extended, tile_pos * TILE, win_width, 1)

    outgoing = jax.vmap(cut_window)(local_pos)
    outgoing = jnp.where(present[:, None, None], outgoing, jnp.zeros((), jnp.bfloat16))
    incoming = route_windows(outgoing)
    windows = jnp.where(
        filled[:, None, None], jnp.take(incoming, source_of, axis=0), jnp.zeros((), jnp.bfloat16)
    )
    summed = lax.psum_scatter(
        segment_terms(windows, seg_rows).astype(jnp.bfloat16), "tm", scatter_dimension=0, tiled=True
    ).astype(jnp.float32)
    scaled = summed * lax.rsqrt(jnp.float32(total_time))
    return scaled.reshape((1,) + scaled.shape)


def solution(mesh):
    return jax.shard_map(
        shards,
        mesh=mesh,
        in_specs=(P("tm", ("rowblk", "colblk")), P()),
        out_specs=P(("rowblk", "colblk"), "tm", None, None, None),
        check_vma=False,
    )
```

profile of v0, /device:TPU:1, one launch (start us, length us, event | category | flops | bytes accessed | tf_op | source)
XLA Modules:
  0.0 1010.7 jit_solution(14492238036259679840)
XLA Ops:
  8.3 18.2 %psum.7 = f32[1024]{0:T(1024)S(1)} all-reduce(f32[1024]{0:T(1024)S(1)} %fusion.16), channel_id=1, replica_groups=mesh['tm'=8,'rowblk'=4,'colblk'=4] {'tm'}, use_global_device_ids=true, to_apply=%region_6.7 | all-reduce | flops 1024 | bytes 8192 | tf_op jit(solution)/shard_map/psum | solution.py:44
  28.4 8.8 collective-permute-start
  38.0 6.0 collective-permute-done
  45.3 3.2 collective-permute-done.1
  50.0 58.8 %while.2 = (s32[]{:T(128)}, bf16[775,1408]{1,0:T(8,128)(2,1)}, s32[16,2]{0,1:T(2,128)S(1)}, bf16[16,775,512]{2,1,0:T(8,128)(2,1)}) while((s32[]{:T(128)}, bf16[775,1408]{1,0:T(8,128)(2,1)}, s32[16,2]{0,1:T(2,128)S(1)}, bf16[16,775,512]{2,1,0:T(8,128)(2,1)}) %tuple.19), condition=%wide.while_cond.clone, body=%wide.while_body.sunk.clone | while | flops 2 | bytes 1590353 | solution.py:66
  50.6 3.0 bitcast_dynamic-update-slice_fusion.11
  57.9 3.1 bitcast_dynamic-update-slice_fusion.11
  61.6 3.1 bitcast_dynamic-update-slice_fusion.11
  68.9 3.1 bitcast_dynamic-update-slice_fusion.11
  72.6 3.1 bitcast_dynamic-update-slice_fusion.11
  76.2 3.1 bitcast_dynamic-update-slice_fusion.11
  79.9 3.0 bitcast_dynamic-update-slice_fusion.11
  83.6 3.0 bitcast_dynamic-update-slice_fusion.11
  87.2 3.1 bitcast_dynamic-update-slice_fusion.11
  91.0 3.1 bitcast_dynamic-update-slice_fusion.11
  98.4 3.1 bitcast_dynamic-update-slice_fusion.11
  102.1 3.0 bitcast_dynamic-update-slice_fusion.11
  105.8 3.1 bitcast_dynamic-update-slice_fusion.11
  108.8 10.7 %broadcast_select_fusion = bf16[16,775,512]{2,1,0:T(8,128)(2,1)} fusion(bf16[16,775,512]{2,1,0:T(8,128)(2,1)} %get-tuple-element.12, pred[16]{0:T(512)(128)(4,1)S(1)} %fusion.44), kind=kLoop, calls=%fused_computation.4 | loop fusion | flops 6348800 | bytes 25395216 | tf_op jit(solution)/shard_map/jit(_where)/select_n | solution.py:69
  119.6 12.9 %all-to-all-start = ((bf16[16,775,512]{2,1,0:T(8,128)(2,1)}), bf16[16,775,512]{2,1,0:T(8,128)(2,1)}, u32[]{:S(2)}, u32[]{:S(2)}) async-start(bf16[16,775,512]{2,1,0:T(8,128)(2,1)} %broadcast_select_fusion), calls=%async_computation | async-start | bytes 25427968 | tf_op jit(solution)/shard_map/all_to_all | solution.py:30
  133.2 161.5 %all-to-all-done = bf16[16,775,512]{2,1,0:T(8,128)(2,1)} async-done(((bf16[16,775,512]{2,1,0:T(8,128)(2,1)}), bf16[16,775,512]{2,1,0:T(8,128)(2,1)}, u32[]{:S(2)}, u32[]{:S(2)}) %all-to-all-start) | async-done | bytes 12697632 | tf_op jit(solution)/shard_map/all_to_all | solution.py:30
  294.6 11.2 %gather_fusion = bf16[16,775,512]{2,1,0:T(8,128)(2,1)} fusion(bf16[16,775,512]{2,1,0:T(8,128)(2,1)} %all-to-all-done, s32[1024]{0:T(1024)S(1)} %pad_clamp_fusion), kind=kCustom, calls=%fused_computation | custom fusion | bytes 25395264 | tf_op jit(solution)/shard_map/jit(_take)/gather | solution.py:72
  305.8 6.8 select_select_fusion
  312.6 3.3 bitcast_dynamic-update-slice_fusion.8
  315.9 4.7 bitcast_dynamic-update-slice_fusion.7
  320.6 4.8 bitcast_dynamic-update-slice_fusion.6
  325.3 4.7 bitcast_dynamic-update-slice_fusion.5
  330.1 4.7 bitcast_dynamic-update-slice_fusion.4
  334.8 4.7 bitcast_dynamic-update-slice_fusion.3
  339.5 4.7 bitcast_dynamic-update-slice_fusion.2
  344.2 4.7 bitcast_dynamic-update-slice_fusion.1
  350.8 648.1 %all-reduce.4.cloned.1.call-done = bf16[16,8,128,512]{3,2,0,1:T(8,128)(2,1)} async-done(((bf16[16,8,128,512]{3,2,0,1:T(8,128)(2,1)}), bf16[16,8,128,512]{3,2,0,1:T(8,128)(2,1)}) %all-reduce.4.cloned.1.call-update) | async-done | bytes 16777232
  (66 shorter events, 33.1 us)
Async XLA Ops:
  28.4 15.6 %collective-permute-start = (bf16[768,384]{1,0:T(8,128)(2,1)S(1)}, bf16[768,384]{1,0:T(8,128)(2,1)S(1)}, u32[]{:S(2)}, u32[]{:S(2)}) collective-permute-start(bf16[768,384]{1,0:T(8,128)(2,1)S(1)} %slice.57), channel_id=1, source_target_pairs={{1,0},{2,1},{3,2},{4,3},{5,4},{6,5},{7,6},{8,7},{9,8},{10,9},{11,1... | collective-permute-start | bytes 1769480 | tf_op jit(solution)/shard_map/ppermute | solution.py:15
  44.0 4.5 collective-permute-start.1
  119.6 175.1 %all-to-all-start = ((bf16[16,775,512]{2,1,0:T(8,128)(2,1)}), bf16[16,775,512]{2,1,0:T(8,128)(2,1)}, u32[]{:S(2)}, u32[]{:S(2)}) async-start(bf16[16,775,512]{2,1,0:T(8,128)(2,1)} %broadcast_select_fusion), calls=%async_computation | async-start | bytes 25427968 | tf_op jit(solution)/shard_map/all_to_all | solution.py:30
  132.5 866.4 %all-reduce.4.cloned.1.call-start = ((), (), s32[]{:S(2)}) async-start(), calls=%async_computation.1 | async-start | bytes 33554432
  348.9 0.7 copy-start
Sparse Core Ops, SparseCore 0:
  349.1 649.8 all-reduce.3
where the time goes:
time: 1010 us
  waiting for transfers between devices  819 us (81%)
  local copies, waits for them, and re-layouts  74.8 us (7%)
  matrix products  36.3 us (4%)
  other arithmetic  25.5 us (3%)
  starting transfers between devices  23 us (2%)
  blocking collectives  18.2 us (2%)
  between operations  14.1 us (1%)
    unnamed x2, waiting for transfers between devices  648 us
    all_to_all x1, waiting for transfers between devices, route_windows(): lax.all_to_all(outgoing, ('rowblk', 'colblk'), split_axis=0, concat_axis=...  161 us
    gather x48, local copies, waits for them, and re-layouts  58.8 us
    dot_general x8, matrix products, segment_terms(): jnp.einsum('kti,ktc->kic', first_tile, second, preferred_element_type=jnp...  36.3 us
  transfers between devices with their start and end apart: 4, of which 4 were waited for; matrix products, arithmetic and copies ran while one was open for 0% of the time, Pallas kernels for 0%

commit v1 on v0

v1 whole, which is shorter than its diff:
```python
import jax
import jax.numpy as jnp
from jax import lax
from jax.sharding import PartitionSpec as P

TILE = 128
LAGS = 8
APER = 3
OCAP = 16


def passed_along(block, axis, distance):
    devices = range(lax.axis_size(axis))
    route = [(i - distance, i) for i in devices if i - distance in devices]
    return lax.ppermute(block, axis, route)


def shards(signal, tile_owner):
    seg_rows, local_width = signal.shape
    tiles_here = local_width // TILE
    owners = lax.axis_size(("rowblk", "colblk"))
    segments = lax.axis_size("tm")
    total_time = seg_rows * segments
    win_width = (APER + 1) * TILE
    values = signal.astype(jnp.float32)
    power_sum = lax.psum(jnp.sum(values * values, axis=0), "tm")
    normed = (values * lax.rsqrt(power_sum / total_time + 1e-06)).astype(jnp.bfloat16)
    following = passed_along(normed[:, : APER * TILE], ("rowblk", "colblk"), -1)
    extended = jnp.concatenate([normed, following], axis=1)
    my_index = lax.axis_index(("rowblk", "colblk"))
    owner_table = tile_owner.reshape(owners, tiles_here)
    my_owners = lax.dynamic_index_in_dim(owner_table, my_index, 0, keepdims=False)
    targets = jnp.arange(owners, dtype=jnp.int32)
    matches = my_owners[None, :] == targets[:, None]
    local_pos = jnp.sum(
        jnp.where(matches, jnp.arange(tiles_here, dtype=jnp.int32)[None, :], 0), axis=1
    )
    arrived = jnp.any(owner_table == my_index, axis=1)
    slot_rank = jnp.cumsum(arrived.astype(jnp.int32)) - 1
    picker = (slot_rank[None, :] == jnp.arange(OCAP, dtype=jnp.int32)[:, None]) & arrived[None, :]
    source_of = jnp.sum(jnp.where(picker, targets[None, :], 0), axis=1)
    filled = jnp.any(picker, axis=1)

    windows = jnp.stack(
        [extended[:, a * TILE : a * TILE + win_width] for a in range(tiles_here)], axis=0
    )
    window = lax.all_to_all(windows, "tm", split_axis=0, concat_axis=0, tiled=True)
    window = window.reshape(total_time, win_width)
    later = jnp.pad(window, ((0, LAGS - 1), (0, 0)))
    first = window[:, :TILE]
    result = jnp.stack(
        [
            jnp.einsum(
                "ti,tc->ic", first, later[l : l + total_time], preferred_element_type=jnp.float32
            )
            for l in range(LAGS)
        ],
        axis=0,
    )
    result = (result * lax.rsqrt(jnp.float32(total_time))).astype(jnp.bfloat16)
    by_lag = lax.all_to_all(result, "tm", split_axis=0, concat_axis=0, tiled=True)
    outgoing = jnp.take(by_lag, local_pos, axis=0)
    incoming = lax.all_to_all(
        outgoing, ("rowblk", "colblk"), split_axis=0, concat_axis=0, tiled=True
    )
    slots = jnp.where(
        filled[:, None, None], jnp.take(incoming, source_of, axis=0), jnp.zeros((), jnp.bfloat16)
    )
    mine = lax.all_to_all(slots, "tm", split_axis=0, concat_axis=0, tiled=True)
    mine = mine.reshape(LAGS, OCAP // segments, TILE, win_width).transpose(1, 0, 2, 3)
    return mine.astype(jnp.float32)[None]


def solution(mesh):
    return jax.shard_map(
        shards,
        mesh=mesh,
        in_specs=(P("tm", ("rowblk", "colblk")), P()),
        out_specs=P(("rowblk", "colblk"), "tm", None, None, None),
        check_vma=False,
    )
```

time: 1010 us -> 222 us (0.22)
  waiting for transfers between devices: 819 us -> 47.5 us
  blocking collectives: 18.2 us -> 118 us
  local copies, waits for them, and re-layouts: 74.8 us -> 3.56 us
  matrix products: 36.3 us -> 15.3 us
  other arithmetic: 25.5 us -> 8.91 us
  between operations: 14.1 us -> 0.23 us
    unnamed x2 -> x0, waiting for transfers between devices: 648 us -> none
    all_to_all x1 -> x2, waiting for transfers between devices: 161 us -> 41.1 us  [the longest x1 28.5 us: shards(): lax.all_to_all(outgoing, ('rowblk', 'colblk'), split_axis=0, concat_axis=...]
    all_to_all x0 -> x2, blocking collectives: none -> 100 us  [the longest x1 73 us: shards(): lax.all_to_all(windows, 'tm', split_axis=0, concat_axis=0, tiled=True)]
    gather x48 -> x1, local copies, waits for them, and re-layouts: 58.8 us -> 0.68 us  [shards(): outgoing = jnp.take(by_lag, local_pos, axis=0)]
    dot_general x8, matrix products: 36.3 us -> 15.3 us  [shards(): jnp.einsum('ti,tc->ic', first, later[l:l + total_time], preferred_element...]
  transfers between devices with their start and end apart: 4 -> 3, of which waited for: 4 -> 3; matrix products, arithmetic and copies ran while one was open for 0% -> 1% of each run, Pallas kernels for 0% -> 0%
where the time goes in v1:
time: 222 us; the launch traced here: 220 us
  blocking collectives  118 us (53%)
  waiting for transfers between devices  47.5 us (21%)
  starting transfers between devices  25.8 us (12%)
  matrix products  15.3 us (7%)
  other arithmetic  8.91 us (4%)
  local copies, waits for them, and re-layouts  3.56 us (2%)
    all_to_all x1, blocking collectives, shards(): lax.all_to_all(windows, 'tm', split_axis=0, concat_axis=0, tiled=True)  73 us
    all_to_all x1, waiting for transfers between devices, shards(): lax.all_to_all(outgoing, ('rowblk', 'colblk'), split_axis=0, concat_axis=...  28.5 us
    all_to_all x1, blocking collectives, shards(): mine = lax.all_to_all(slots, 'tm', split_axis=0, concat_axis=0, tiled=True)  27.3 us
    psum x1, blocking collectives, shards(): power_sum = lax.psum(jnp.sum(values * values, axis=0), 'tm')  18.2 us
    dot_general x8, matrix products, shards(): jnp.einsum('ti,tc->ic', first, later[l:l + total_time], preferred_element...  15.3 us
    all_to_all x1, starting transfers between devices, shards(): lax.all_to_all(outgoing, ('rowblk', 'colblk'), split_axis=0, concat_axis=...  13.5 us
    all_to_all x1, waiting for transfers between devices, shards(): lax.all_to_all(result, 'tm', split_axis=0, concat_axis=0, tiled=True)  12.5 us
    ppermute x1, starting transfers between devices, passed_along(): return lax.ppermute(block, axis, route)  8.77 us
  transfers between devices with their start and end apart: 3, of which 3 were waited for; matrix products, arithmetic and copies ran while one was open for 1% of the time, Pallas kernels for 0%

profile of v1, /device:TPU:1, one launch (start us, length us, event | category | flops | bytes accessed | tf_op | source)
XLA Modules:
  0.0 219.8 jit_solution(746119176087796177)
XLA Ops:
  0.0 1.9 fusion.14
  1.9 18.2 %psum.7 = f32[1024]{0:T(1024)S(1)} all-reduce(f32[1024]{0:T(1024)S(1)} %fusion.14), channel_id=1, replica_groups=mesh['tm'=8,'rowblk'=4,'colblk'=4] {'tm'}, use_global_device_ids=true, to_apply=%region_6.7 | all-reduce | flops 1024 | bytes 8192 | tf_op jit(solution)/shard_map/psum | solution.py:26
  20.1 0.4 fusion.15
  20.5 8.8 %collective-permute-start = (bf16[768,384]{1,0:T(8,128)(2,1)S(1)}, bf16[768,384]{1,0:T(8,128)(2,1)S(1)}, u32[]{:S(2)}, u32[]{:S(2)}) collective-permute-start(bf16[768,384]{1,0:T(8,128)(2,1)S(1)} %slice.78), channel_id=1, source_target_pairs={{1,0},{2,1},{3,2},{4,3},{5,4},{6,5},{7,6},{8,7},{9,8},{10,9},{11,1... | collective-permute-start | bytes 1769480 | tf_op jit(solution)/shard_map/ppermute | solution.py:15
  29.7 6.4 %collective-permute-done = bf16[768,384]{1,0:T(8,128)(2,1)S(1)} collective-permute-done((bf16[768,384]{1,0:T(8,128)(2,1)S(1)}, bf16[768,384]{1,0:T(8,128)(2,1)S(1)}, u32[]{:S(2)}, u32[]{:S(2)}) %collective-permute-start) | collective-permute-done | bytes 589856 | tf_op jit(solution)/shard_map/ppermute | solution.py:15
  36.1 0.1 fusion.71
  36.3 0.1 fusion.73
  36.4 73.0 %all_to_all.20 = bf16[8,768,512]{2,1,0:T(8,128)(2,1)S(1)} all-to-all(bf16[8,768,512]{2,1,0:T(8,128)(2,1)S(1)} %fusion.73), channel_id=1, replica_groups=mesh['tm'=8,'rowblk'=4,'colblk'=4] {'tm'}, dimensions={0} | all-to-all | bytes 12582912 | tf_op jit(solution)/shard_map/all_to_all | solution.py:47
  109.4 1.0 fusion.65
  110.4 2.0 fusion.26
  112.4 2.0 fusion.32
  114.5 2.0 fusion.38
  116.6 2.0 fusion.44
  118.6 2.0 fusion.50
  120.7 2.0 fusion.56
  122.7 2.0 fusion.62
  124.8 1.2 multiply_convert_fusion
  126.0 3.6 %all-to-all-start.1 = ((bf16[8,128,512]{2,1,0:T(8,128)(2,1)}), bf16[8,128,512]{2,1,0:T(8,128)(2,1)S(1)}, u32[]{:S(2)}, u32[]{:S(2)}) async-start(bf16[8,128,512]{2,1,0:T(8,128)(2,1)} %multiply_convert_fusion), calls=%async_computation.1 | async-start | bytes 2097152 | tf_op jit(solution)/shard_map/all_to_all | solution.py:61
  129.8 12.5 %all-to-all-done.1 = bf16[8,128,512]{2,1,0:T(8,128)(2,1)S(1)} async-done(((bf16[8,128,512]{2,1,0:T(8,128)(2,1)}), bf16[8,128,512]{2,1,0:T(8,128)(2,1)S(1)}, u32[]{:S(2)}, u32[]{:S(2)}) %all-to-all-start.1) | async-done | bytes 1048608 | tf_op jit(solution)/shard_map/all_to_all | solution.py:61
  142.4 0.7 gather_fusion
  143.1 1.6 broadcast_select_fusion
  144.7 13.5 %all-to-all-start.2 = ((bf16[16,128,512]{2,1,0:T(8,128)(2,1)}), bf16[16,128,512]{2,1,0:T(8,128)(2,1)}, u32[]{:S(2)}, u32[]{:S(2)}) async-start(bf16[16,128,512]{2,1,0:T(8,128)(2,1)} %broadcast_select_fusion), calls=%async_computation.2 | async-start | bytes 4194304 | tf_op jit(solution)/shard_map/all_to_all | solution.py:63
  158.1 0.1 compare_reduce_fusion
  158.2 0.1 copy.7
  158.4 0.1 add_reduce_fusion
  158.5 0.1 select_reduce_fusion
  158.6 0.1 fusion.88
  158.7 28.5 %all-to-all-done.2 = bf16[16,128,512]{2,1,0:T(8,128)(2,1)} async-done(((bf16[16,128,512]{2,1,0:T(8,128)(2,1)}), bf16[16,128,512]{2,1,0:T(8,128)(2,1)}, u32[]{:S(2)}, u32[]{:S(2)}) %all-to-all-start.2) | async-done | bytes 2097184 | tf_op jit(solution)/shard_map/all_to_all | solution.py:63
  187.2 2.3 %gather_fusion.1 = bf16[16,128,512]{2,1,0:T(8,128)(2,1)S(1)} fusion(bf16[16,128,512]{2,1,0:T(8,128)(2,1)} %all-to-all-done.2, s32[1024]{0:T(1024)S(1)} %pad_clamp_fusion), kind=kCustom, calls=%fused_computation.1 | custom fusion | bytes 4194368 | tf_op jit(solution)/shard_map/jit(_take)/gather | solution.py:67
  189.5 0.3 select_select_fusion
  189.8 27.3 %all_to_all.21 = bf16[16,128,512]{2,1,0:T(8,128)(2,1)S(1)} all-to-all(bf16[16,128,512]{2,1,0:T(8,128)(2,1)S(1)} %select_select_fusion), channel_id=1, replica_groups=mesh['tm'=8,'rowblk'=4,'colblk'=4] {'tm'}, dimensions={0} | all-to-all | bytes 4194304 | tf_op jit(solution)/shard_map/all_to_all | solution.py:69
  217.2 2.6 %copy_bitcast_fusion = f32[1,2,8,128,512]{4,3,2,1,0:T(8,128)} fusion(bf16[8,2,128,512]{3,2,1,0:T(8,128)(2,1)S(1)} %bitcast.92), kind=kLoop, calls=%fused_computation.16 | loop fusion | flops 1048576 | bytes 6291456 | tf_op jit(solution)/shard_map/broadcast_in_dim | solution.py:71
  (23 shorter events, 0.8 us)
Async XLA Ops:
  0.0 20.1 %copy-start = (bf16[768,1024]{1,0:T(8,128)(2,1)S(1)}, bf16[768,1024]{1,0:T(8,128)(2,1)}, u32[]{:S(2)}) copy-start(bf16[768,1024]{1,0:T(8,128)(2,1)} %param.2) | copy-start | bytes 4718596
  20.5 15.6 %collective-permute-start = (bf16[768,384]{1,0:T(8,128)(2,1)S(1)}, bf16[768,384]{1,0:T(8,128)(2,1)S(1)}, u32[]{:S(2)}, u32[]{:S(2)}) collective-permute-start(bf16[768,384]{1,0:T(8,128)(2,1)S(1)} %slice.78), channel_id=1, source_target_pairs={{1,0},{2,1},{3,2},{4,3},{5,4},{6,5},{7,6},{8,7},{9,8},{10,9},{11,1... | collective-permute-start | bytes 1769480 | tf_op jit(solution)/shard_map/ppermute | solution.py:15
  124.8 4.8 %copy-start.1 = (s32[128]{0:T(128)S(1)}, s32[128]{0:T(128)}, u32[]{:S(2)}) copy-start(s32[128]{0:T(128)} %param.3) | copy-start | bytes 1540
  126.0 16.3 %all-to-all-start.1 = ((bf16[8,128,512]{2,1,0:T(8,128)(2,1)}), bf16[8,128,512]{2,1,0:T(8,128)(2,1)S(1)}, u32[]{:S(2)}, u32[]{:S(2)}) async-start(bf16[8,128,512]{2,1,0:T(8,128)(2,1)} %multiply_convert_fusion), calls=%async_computation.1 | async-start | bytes 2097152 | tf_op jit(solution)/shard_map/all_to_all | solution.py:61
  144.7 42.6 %all-to-all-start.2 = ((bf16[16,128,512]{2,1,0:T(8,128)(2,1)}), bf16[16,128,512]{2,1,0:T(8,128)(2,1)}, u32[]{:S(2)}, u32[]{:S(2)}) async-start(bf16[16,128,512]{2,1,0:T(8,128)(2,1)} %broadcast_select_fusion), calls=%async_computation.2 | async-start | bytes 4194304 | tf_op jit(solution)/shard_map/all_to_all | solution.py:63

commit v2 on v1

v2 whole, which is shorter than its diff:
```python
import functools

import jax
import jax.numpy as jnp
from jax import lax
from jax.experimental import pallas as pl
from jax.experimental.pallas import tpu as pltpu
from jax.sharding import PartitionSpec as P

MESH = pl.DeviceIdType.MESH
TILE = 128
LAGS = 8
APER = 3
OCAP = 16
BLOCKS = 16
SEGS = 8
ROWS = 768
WIN = 512
HALF = 256
HALO = 16
PRESCALE = 2.0**40


def kernel(
    pos_ref, src_ref, fill_ref, sig_ref, out_ref,
    ybuf, halo, amat, acc, pow_mine, pow_other, send_y, recv_y, send_z,
    piece_a, piece_b, send_o, recv_o_a, recv_o_b, send_t,
    g_send, g_recv, h_send, h_recv, p_send, p_recv, y_send, y_recv,
    z_send, z_recv, o_send, o_recv, t_send, t_recv,
):
    t = lax.axis_index("tm")
    row = lax.axis_index("rowblk")
    col = lax.axis_index("colblk")
    b = row * 4 + col
    z = t // 2
    yl = t % 2

    piece = (piece_a, piece_b)
    recv_o = (recv_o_a, recv_o_b)

    def dev(block, tm):
        return (tm, block // 4, block % 4)

    barrier = pltpu.get_barrier_semaphore()
    for d in range(1, SEGS):
        pl.semaphore_signal(barrier, inc=1, device_id=dev(b, (t + d) % SEGS), device_id_type=MESH)
    for d in range(1, BLOCKS):
        pl.semaphore_signal(barrier, inc=1, device_id=dev((b + d) % BLOCKS, t), device_id_type=MESH)
    for d in (1, BLOCKS - 1):
        for k in range(1, 4):
            pl.semaphore_signal(
                barrier, inc=1, device_id=dev((b + d) % BLOCKS, (t + 2 * k) % SEGS), device_id_type=MESH
            )
    pl.semaphore_wait(barrier, SEGS - 1 + BLOCKS - 1 + 6)

    def window_copy(k, c):
        zd = (z + k) % 4
        tile = 2 * zd + c
        block = (b + BLOCKS - tile // 8) % BLOCKS
        src = sig_ref.at[:, pl.ds(pl.multiple_of((tile % 8) * TILE, TILE), TILE)]
        dst = ybuf.at[z, :, pl.ds(c * TILE, TILE)]
        return src, dst, block, zd

    def start_window(k, c):
        src, dst, block, zd = window_copy(k, c)
        pltpu.make_async_remote_copy(
            src_ref=src, dst_ref=dst, send_sem=g_send.at[k, c], recv_sem=g_recv.at[z, c],
            device_id=dev(block, 2 * zd + yl), device_id_type=MESH,
        ).start()

    def local_window(c):
        src, dst, _, _ = window_copy(0, c)
        return pltpu.make_async_copy(src, dst, g_recv.at[z, c])

    def wait_window_recv(s, c):
        dst = ybuf.at[s, :, pl.ds(c * TILE, TILE)]
        pltpu.make_async_remote_copy(
            src_ref=dst, dst_ref=dst, send_sem=g_send.at[0, c], recv_sem=g_recv.at[s, c],
            device_id=dev(b, (t + 1) % SEGS), device_id_type=MESH,
        ).wait_recv()

    def wait_window_send(k, c):
        src, dst, block, zd = window_copy(k, c)
        pltpu.make_async_remote_copy(
            src_ref=src, dst_ref=dst, send_sem=g_send.at[k, c], recv_sem=g_recv.at[z, c],
            device_id=dev((b + 1) % BLOCKS, 2 * zd + yl), device_id_type=MESH,
        ).wait_send()

    def own(c):
        return 2 * z + c < 8

    def start_windows(tiles):
        for c in tiles:
            for k in (2, 1, 3):
                start_window(k, c)
            if c < 2:
                local_window(c).start()
            else:
                pl.when(own(c))(lambda c=c: local_window(c).start())
                pl.when(jnp.logical_not(own(c)))(lambda c=c: start_window(0, c))

    def wait_windows(k, tiles):
        s = (z + k) % 4
        for c in tiles:
            if k == 0:
                if c < 2:
                    local_window(c).wait()
                else:
                    pl.when(own(c))(lambda c=c: local_window(c).wait())
                    pl.when(jnp.logical_not(own(c)))(lambda c=c: wait_window_recv(s, c))
            else:
                wait_window_recv(s, c)

    def halo_copy(k):
        zd = (z + k) % 4
        slot = (z + yl) % 4
        return pltpu.make_async_remote_copy(
            src_ref=sig_ref.at[pl.ds(ROWS - HALO, HALO), pl.ds(pl.multiple_of(zd * HALF, HALF), HALF)],
            dst_ref=halo.at[slot], send_sem=h_send.at[k], recv_sem=h_recv.at[slot],
            device_id=dev(b, 2 * zd + 1 - yl), device_id_type=MESH,
        )

    def wait_halo(s):
        pltpu.make_async_remote_copy(
            src_ref=halo.at[s], dst_ref=halo.at[s], send_sem=h_send.at[0], recv_sem=h_recv.at[s],
            device_id=dev(b, (t + 1) % SEGS), device_id_type=MESH,
        ).wait_recv()

    for k in range(4):
        halo_copy(k).start()
    start_windows((0, 1, 2))
    start_windows((3, 4))

    def square_sums(s, part):
        first, width = (0, 3 * TILE) if part == 0 else (3 * TILE, 2 * TILE)
        v = ybuf[s, :, first : first + width].astype(jnp.float32)
        total = jnp.sum((v * v).reshape(ROWS // 8, 8, width), axis=0)
        pow_mine[part, :, 0:width] = pow_mine[part, :, 0:width] + total

    def build_lags(s):
        keep = jnp.where(jnp.logical_and(s == 0, yl == 0), 0.0, PRESCALE)
        for a in range(2):
            x = ybuf[s, :, a * TILE : (a + 1) * TILE].astype(jnp.float32) * PRESCALE
            h = halo[s, :, a * TILE : (a + 1) * TILE].astype(jnp.float32) * keep
            rows = jnp.concatenate([jnp.zeros((TILE - HALO, TILE), jnp.float32), h, x], axis=0)
            cols = jnp.transpose(rows)
            for j in range(LAGS):
                shifted = cols if j == 0 else pltpu.roll(cols, j, 1)
                amat[s, a, j * TILE : (j + 1) * TILE, :] = shifted[:, TILE:].astype(jnp.bfloat16)

    def products(s, part, first):
        for a in range(2):
            y = ybuf[s, :, (a + 2 * part) * TILE : (a + 2 * part + 2) * TILE]
            for j in range(0, LAGS, 2):
                p = jnp.dot(
                    amat[s, a, j * TILE : (j + 2) * TILE, :], y, preferred_element_type=jnp.float32
                ).reshape(2, TILE, HALF)
                if first:
                    acc[part, a, j : j + 2] = p
                else:
                    acc[part, a, j : j + 2] = acc[part, a, j : j + 2] + p

    pow_mine[...] = jnp.zeros_like(pow_mine)

    def partner_power(part):
        return pltpu.make_async_remote_copy(
            src_ref=pow_mine.at[part], dst_ref=pow_other.at[part], send_sem=p_send.at[part],
            recv_sem=p_recv.at[part], device_id=dev(b, 2 * z + 1 - yl), device_id_type=MESH,
        )

    def partner_terms(part):
        return pltpu.make_async_remote_copy(
            src_ref=send_y.at[part], dst_ref=recv_y.at[part], send_sem=y_send.at[part],
            recv_sem=y_recv.at[part], device_id=dev(b, 2 * z + 1 - yl), device_id_type=MESH,
        )

    def start_partner(part):
        partner_power(part).start()
        for a in range(2):
            for q in range(4):
                send_y[part, a, q] = acc[part, a, 2 * q + 1 - yl].astype(jnp.bfloat16)
        partner_terms(part).start()

    def channel_scale(part):
        total = jnp.sum(pow_mine[part] + pow_other[part], axis=0, keepdims=True)
        return lax.rsqrt(total * (1.0 / (SEGS * ROWS)) + 1e-06)

    def piece_copy(part, k):
        zd = (z + k) % 4
        return pltpu.make_async_remote_copy(
            src_ref=send_z.at[part, zd], dst_ref=piece[part].at[pl.ds(2 * z, 2)],
            send_sem=z_send.at[part, k], recv_sem=z_recv.at[part, z],
            device_id=dev(b, 2 * zd + yl), device_id_type=MESH,
        )

    def wait_piece(part, k):
        s = (z + k) % 4
        pltpu.make_async_remote_copy(
            src_ref=send_z.at[part, s], dst_ref=piece[part].at[pl.ds(2 * s, 2)],
            send_sem=z_send.at[part, k], recv_sem=z_recv.at[part, s],
            device_id=dev(b, 2 * s + yl), device_id_type=MESH,
        ).wait_recv()

    def start_pieces(part):
        partner_power(part).wait_recv()
        scales = channel_scale(part)
        if part == 0:
            low = scales
            wide = scales
        else:
            low = channel_scale(0)
            wide = jnp.concatenate([low[:, 2 * TILE :], scales[:, : 2 * TILE]], axis=1)
        first = 2 * z + 2 * part
        lane_tile = lax.broadcasted_iota(jnp.int32, (1, 3 * TILE), 1) // TILE + first
        last_block = jnp.broadcast_to(b, (1, 3 * TILE)) == BLOCKS - 1
        wide = jnp.where(jnp.logical_and(lane_tile >= 8, last_block), 0.0, wide)
        norm = (1.0 / PRESCALE) * float(SEGS * ROWS) ** -0.5
        partner_terms(part).wait_recv()
        for a in range(2):
            rows_scale = jnp.transpose(
                jnp.broadcast_to(low[:, a * TILE : (a + 1) * TILE] * norm, (TILE, TILE))
            )
            rows_scale = jnp.concatenate([rows_scale, rows_scale], axis=1)
            both = rows_scale * wide[:, a * TILE : (a + 2) * TILE]
            for q in range(4):
                total = acc[part, a, 2 * q + yl] + recv_y[part, a, q].astype(jnp.float32)
                send_z[part, q, a] = (total * both).astype(jnp.bfloat16)
        for k in (2, 1, 3):
            piece_copy(part, k).start()
        piece[part][pl.ds(2 * z, 2)] = send_z[part, z]

    def owner_copy(part, d):
        o = (b + d) % BLOCKS
        return pltpu.make_async_remote_copy(
            src_ref=send_o.at[part, d], dst_ref=recv_o[part].at[b], send_sem=o_send.at[part, d],
            recv_sem=o_recv.at[part, b], device_id=dev(o, t), device_id_type=MESH,
        )

    def wait_owner(part, d):
        s = (b + d) % BLOCKS
        pltpu.make_async_remote_copy(
            src_ref=send_o.at[part, d], dst_ref=recv_o[part].at[s], send_sem=o_send.at[part, d],
            recv_sem=o_recv.at[part, s], device_id=dev(s, t), device_id_type=MESH,
        ).wait_recv()

    def start_owners(part):
        for k in (1, 3, 2):
            wait_piece(part, k)

        def send(d, _):
            o = (b + d) % BLOCKS
            send_o[part, d] = piece[part][pos_ref[o]]
            owner_copy(part, d).start()
            return 0

        lax.fori_loop(1, BLOCKS, send, 0)
        recv_o[part][b] = piece[part][pos_ref[b]]

    def slot_dst(part, lag):
        return out_ref.at[:, lag, :, pl.ds(part * HALF, HALF)]

    def slot_copy(part, d):
        return pltpu.make_async_remote_copy(
            src_ref=send_t.at[part, d], dst_ref=slot_dst(part, t), send_sem=t_send.at[part, d],
            recv_sem=t_recv.at[part, t], device_id=dev(b, (t + d) % SEGS), device_id_type=MESH,
        )

    def own_slots(part):
        return pltpu.make_async_copy(send_t.at[part, 0], slot_dst(part, t), t_recv.at[part, t])

    def wait_slots(part, d):
        s = (t + d) % SEGS
        pltpu.make_async_remote_copy(
            src_ref=send_t.at[part, d], dst_ref=slot_dst(part, s), send_sem=t_send.at[part, d],
            recv_sem=t_recv.at[part, s], device_id=dev(b, s), device_id_type=MESH,
        ).wait_recv()

    def start_slots(part):
        def arrive(d, _):
            wait_owner(part, d)
            return 0

        lax.fori_loop(1, BLOCKS, arrive, 0)

        def fill(d):
            base = 2 * ((t + d) % SEGS)
            for e in range(2):
                taken = recv_o[part][src_ref[base + e]]
                keep = jnp.broadcast_to(fill_ref[base + e], (TILE, HALF)) > 0
                send_t[part, d, e] = jnp.where(keep, taken.astype(jnp.float32), 0.0).astype(jnp.bfloat16)

        def send(d, _):
            fill(d)
            slot_copy(part, d).start()
            return 0

        lax.fori_loop(1, SEGS, send, 0)
        fill(0)
        own_slots(part).start()

    for k in (0, 1, 3, 2):
        s = (z + k) % 4
        wait_halo(s)
        wait_windows(k, (0, 1, 2))
        build_lags(s)
        products(s, 0, k == 0)
        square_sums(s, 0)
    start_partner(0)
    for k in (0, 1, 3, 2):
        s = (z + k) % 4
        wait_windows(k, (3, 4))
        products(s, 1, k == 0)
        square_sums(s, 1)
    start_partner(1)
    start_pieces(0)
    start_owners(0)
    start_pieces(1)
    start_slots(0)
    start_owners(1)
    start_slots(1)

    for k in range(4):
        halo_copy(k).wait_send()
    for c in range(5):
        for k in (1, 2, 3):
            wait_window_send(k, c)
        if c >= 2:
            pl.when(jnp.logical_not(own(c)))(lambda c=c: wait_window_send(0, c))
    for part in range(2):
        partner_power(part).wait_send()
        partner_terms(part).wait_send()
        for k in (1, 2, 3):
            piece_copy(part, k).wait_send()

        def owner_done(d, _, part=part):
            owner_copy(part, d).wait_send()
            return 0

        lax.fori_loop(1, BLOCKS, owner_done, 0)

        def slot_done(d, _, part=part):
            slot_copy(part, d).wait_send()
            wait_slots(part, d)
            return 0

        lax.fori_loop(1, SEGS, slot_done, 0)
        own_slots(part).wait()


def route(tile_owner):
    owner_table = tile_owner.reshape(BLOCKS, NT_HERE)
    my_index = lax.axis_index(("rowblk", "colblk"))
    my_owners = lax.dynamic_index_in_dim(owner_table, my_index, 0, keepdims=False)
    targets = jnp.arange(BLOCKS, dtype=jnp.int32)
    matches = my_owners[None, :] == targets[:, None]
    local_pos = jnp.sum(
        jnp.where(matches, jnp.arange(NT_HERE, dtype=jnp.int32)[None, :], 0), axis=1
    )
    arrived = jnp.any(owner_table == my_index, axis=1)
    slot_rank = jnp.cumsum(arrived.astype(jnp.int32)) - 1
    picker = (slot_rank[None, :] == jnp.arange(OCAP, dtype=jnp.int32)[:, None]) & arrived[None, :]
    source_of = jnp.sum(jnp.where(picker, targets[None, :], 0), axis=1)
    filled = jnp.any(picker, axis=1).astype(jnp.int32)
    return local_pos, source_of, filled


NT_HERE = 8


def shards(signal, tile_owner):
    local_pos, source_of, filled = route(tile_owner)
    bf16, f32, vmem, dma = jnp.bfloat16, jnp.float32, pltpu.VMEM, pltpu.SemaphoreType.DMA
    out = pl.pallas_call(
        kernel,
        out_shape=jax.ShapeDtypeStruct((2, LAGS, TILE, WIN), bf16),
        in_specs=[pl.BlockSpec(memory_space=pltpu.SMEM)] * 3 + [pl.BlockSpec(memory_space=pl.ANY)],
        out_specs=pl.BlockSpec(memory_space=pl.ANY),
        scratch_shapes=[
            vmem((4, ROWS, 5 * TILE), bf16),
            vmem((4, HALO, HALF), bf16),
            vmem((4, 2, LAGS * TILE, ROWS), bf16),
            vmem((2, 2, LAGS, TILE, HALF), f32),
            vmem((2, 8, 3 * TILE), f32),
            vmem((2, 8, 3 * TILE), f32),
            vmem((2, 2, 4, TILE, HALF), bf16),
            vmem((2, 2, 4, TILE, HALF), bf16),
            vmem((2, 4, 2, TILE, HALF), bf16),
            vmem((8, TILE, HALF), bf16),
            vmem((8, TILE, HALF), bf16),
            vmem((2, BLOCKS, TILE, HALF), bf16),
            vmem((BLOCKS, TILE, HALF), bf16),
            vmem((BLOCKS, TILE, HALF), bf16),
            vmem((2, SEGS, 2, TILE, HALF), bf16),
            dma((4, 5)), dma((4, 5)), dma((4,)), dma((4,)), dma((2,)), dma((2,)), dma((2,)), dma((2,)),
            dma((2, 4)), dma((2, 4)), dma((2, BLOCKS)), dma((2, BLOCKS)), dma((2, SEGS)), dma((2, SEGS)),
        ],
        compiler_params=pltpu.CompilerParams(
            collective_id=0, has_side_effects=True, vmem_limit_bytes=48 * 1024 * 1024
        ),
    )(local_pos, source_of, filled, signal)
    return out.astype(f32)[None]


def solution(mesh):
    return jax.shard_map(
        shards,
        mesh=mesh,
        in_specs=(P("tm", ("rowblk", "colblk")), P()),
        out_specs=P(("rowblk", "colblk"), "tm", None, None, None),
        check_vma=False,
    )
```

time: 222 us -> 141 us (0.64)
  Pallas kernels: 0 us -> 136 us
  blocking collectives: 118 us -> 0 us
  waiting for transfers between devices: 47.5 us -> 0 us
  starting transfers between devices: 25.8 us -> 0 us
  matrix products: 15.3 us -> 0 us
  other arithmetic: 8.91 us -> 3.2 us
    pallas_call x0 -> x1, Pallas kernels: none -> 136 us  [shards(): pl.pallas_call(kernel, out_shape=jax.ShapeDtypeStruct((2, LAGS, TILE, WIN...]
    all_to_all x2 -> x0, blocking collectives: 100 us -> none  [the longest x1 73 us: shards(): lax.all_to_all(windows, 'tm', split_axis=0, concat_axis=0, tiled=True)]
    all_to_all x2 -> x0, waiting for transfers between devices: 41.1 us -> none  [the longest x1 28.5 us: shards(): lax.all_to_all(outgoing, ('rowblk', 'colblk'), split_axis=0, concat_axis=...]
    psum x1 -> x0, blocking collectives: 18.2 us -> none  [shards(): power_sum = lax.psum(jnp.sum(values * values, axis=0), 'tm')]
    all_to_all x2 -> x0, starting transfers between devices: 17 us -> none  [the longest x1 13.5 us: shards(): lax.all_to_all(outgoing, ('rowblk', 'colblk'), split_axis=0, concat_axis=...]
    dot_general x8 -> x0, matrix products: 15.3 us -> none  [shards(): jnp.einsum('ti,tc->ic', first, later[l:l + total_time], preferred_element...]
    ppermute x1 -> x0, starting transfers between devices: 8.77 us -> none  [passed_along(): return lax.ppermute(block, axis, route)]
    ppermute x1 -> x0, waiting for transfers between devices: 6.41 us -> none  [passed_along(): return lax.ppermute(block, axis, route)]
  transfers between devices with their start and end apart: 3 -> 0, of which waited for: 3 -> 0; matrix products, arithmetic and copies ran while one was open for 1% -> 0% of each run, Pallas kernels for 0% -> 0%
where the time goes in v2:
time: 141 us
  Pallas kernels  136 us (96%)
  other arithmetic  3.2 us (2%)
  local copies, waits for them, and re-layouts  2.23 us (2%)
    pallas_call x1, Pallas kernels, shards(): pl.pallas_call(kernel, out_shape=jax.ShapeDtypeStruct((2, LAGS, TILE, WIN...  136 us

profile of v2, /device:TPU:1, one launch (start us, length us, event | category | flops | bytes accessed | tf_op | source)
XLA Modules:
  0.0 141.0 jit_solution(7115632565919827005)
XLA Ops:
  0.0 0.7 reshape.36
  0.7 0.1 compare_reduce_fusion
  0.9 0.1 select_reduce_fusion.1.pos_ref
  1.0 0.1 copy.5
  1.1 0.1 add_reduce_fusion
  1.2 0.1 fusion.1
  1.3 0.1 select_reduce_fusion.src_ref
  1.5 0.0 copy-start
  1.5 1.4 copy-done
  2.9 135.5 %shard_map.28 = bf16[2,8,128,512]{3,2,1,0:T(8,128)(2,1)S(1)} custom-call(s32[16]{0:T(128)S(1)} %select_reduce_fusion.1.pos_ref, s32[16]{0:T(128)S(1)} %select_reduce_fusion.src_ref, s32[16]{0:T(128)S(1)} %convert_element_type.21.fill_ref, bf16[768,1024]{1,0:T(8,128)(2,1)S(1)} %copy-done), custom_call_target="tpu_custom_call" | custom-call | tf_op jit(solution)/shard_map/pallas_call | solution.py:373
  138.4 2.6 %bitcast_convert_fusion = f32[1,2,8,128,512]{4,3,2,1,0:T(8,128)} fusion(bf16[2,8,128,512]{3,2,1,0:T(8,128)(2,1)S(1)} %shard_map.28), kind=kLoop, calls=%fused_computation | loop fusion | flops 1048576 | bytes 6291456 | tf_op jit(solution)/shard_map/broadcast_in_dim | solution.py:401
  (4 shorter events, 0.1 us)
Async XLA Ops:
  1.5 1.4 %copy-start = (bf16[768,1024]{1,0:T(8,128)(2,1)S(1)}, bf16[768,1024]{1,0:T(8,128)(2,1)}, u32[]{:S(2)}) copy-start(bf16[768,1024]{1,0:T(8,128)(2,1)} %sig_ref.1) | copy-start | bytes 4718596

commit v3 on v1

v3 whole, which is shorter than its diff:
```python
import functools

import jax
import jax.numpy as jnp
from jax import lax
from jax.experimental import pallas as pl
from jax.experimental.pallas import tpu as pltpu
from jax.sharding import PartitionSpec as P

MESH = pl.DeviceIdType.MESH
TILE = 128
LAGS = 8
APER = 3
OCAP = 16
BLOCKS = 16
SEGS = 8
ROWS = 768
WIN = 512
HALF = 256
HALO = 16
PRESCALE = 2.0**40
FORWARDS = ()
FIRST_SENDS = ((2, 0), (1, 0), (3, 0), (2, 1), (1, 1), (3, 1))
LATER_SENDS = (
    ((2, 2), (1, 2), (3, 2), (0, 2), (2, 3), (1, 3), (3, 3), (0, 3), (2, 4), (1, 4), (3, 4), (0, 4)), (), (), (), (),
)


def kernel(
    pos_ref, src_ref, fill_ref, sig_ref, out_ref,
    ybuf, halo, following, amat, acc, pow_mine, pow_other, row_scale, send_y, recv_y, send_z,
    piece_0, piece_1, piece_2, piece_3, recv_o_0, recv_o_1, recv_o_2, recv_o_3, send_o, send_t,
    g_send, g_recv, f_send, n_send, n_recv, h_send, h_recv, p_send, p_recv, y_send, y_recv,
    z_send, z_recv, o_send, o_recv, t_send, t_recv,
):
    t = lax.axis_index("tm")
    row = lax.axis_index("rowblk")
    col = lax.axis_index("colblk")
    b = row * 4 + col
    z = t // 2
    yl = t % 2
    piece = (piece_0, piece_1, piece_2, piece_3)
    recv_o = (recv_o_0, recv_o_1, recv_o_2, recv_o_3)

    def dev(block, tm):
        return (tm, block // 4, block % 4)

    def remote(src, dst, send_sem, recv_sem, device):
        return pltpu.make_async_remote_copy(
            src_ref=src, dst_ref=dst, send_sem=send_sem, recv_sem=recv_sem,
            device_id=device, device_id_type=MESH,
        )

    partner = dev(b, 2 * z + 1 - yl)

    barrier = pltpu.get_barrier_semaphore()
    for d in range(1, SEGS):
        pl.semaphore_signal(barrier, inc=1, device_id=dev(b, (t + d) % SEGS), device_id_type=MESH)
    for d, k in ((1, 2), (BLOCKS - 1, SEGS - 2)):
        pl.semaphore_signal(
            barrier, inc=1, device_id=dev((b + d) % BLOCKS, (t + k) % SEGS), device_id_type=MESH
        )
    for d in range(1, BLOCKS):
        pl.semaphore_signal(barrier, inc=1, device_id=dev((b + d) % BLOCKS, t), device_id_type=MESH)

    def window_dst(c):
        return ybuf.at[z, :, pl.ds(c * TILE, TILE)]

    def own_tile(g):
        return sig_ref.at[:, pl.ds(pl.multiple_of(g * TILE, TILE), TILE)]

    def window_copy(k, c, src):
        zd = (z + k) % 4
        return remote(src, window_dst(c), g_send.at[k, c], g_recv.at[z, c], dev(b, 2 * zd + yl))

    def start_window(k, c):
        g = 2 * ((z + k) % 4) + c

        def start(src):
            if k == 0:
                pltpu.make_async_copy(src, window_dst(c), g_recv.at[z, c]).start()
            else:
                window_copy(k, c, src).start()

        if c < 2:
            start(own_tile(g))
        else:
            pl.when(g < 8)(lambda: start(own_tile(g)))
            pl.when(g >= 8)(lambda: start(following.at[g - 8]))

    def wait_window(k, c):
        s = (z + k) % 4
        dst = ybuf.at[s, :, pl.ds(c * TILE, TILE)]
        if k == 0:
            pltpu.make_async_copy(dst, dst, g_recv.at[s, c]).wait()
        else:
            remote(dst, dst, g_send.at[k, c], g_recv.at[s, c], partner).wait_recv()

    def following_copy(i):
        return remote(
            own_tile(i), following.at[i], n_send.at[i], n_recv.at[i], dev((b + BLOCKS - 1) % BLOCKS, t)
        )

    def forward(c):
        step, held = (1, 3) if c == 1 else (3, c - 2)
        s = (z + 3) % 4 if c == 1 else (z + 1) % 4
        zd = (z + step) % 4
        block = (b + (z + step) // 4 + (BLOCKS if c == 1 else BLOCKS - 1)) % BLOCKS
        return remote(
            ybuf.at[s, :, pl.ds(held * TILE, TILE)], ybuf.at[s, :, pl.ds(c * TILE, TILE)],
            f_send.at[c - 1], g_recv.at[s, c], dev(block, 2 * zd + yl),
        )

    def halo_copy(k):
        zd = (z + k) % 4
        slot = (z + yl) % 4
        src = sig_ref.at[pl.ds(ROWS - HALO, HALO), pl.ds(pl.multiple_of(zd * HALF, HALF), HALF)]
        return remote(src, halo.at[slot], h_send.at[k], h_recv.at[slot], dev(b, 2 * zd + 1 - yl))

    def wait_halo(s):
        remote(halo.at[s], halo.at[s], h_send.at[0], h_recv.at[s], partner).wait_recv()

    for c in range(2):
        start_window(0, c)

    pl.semaphore_wait(barrier, SEGS - 1 + BLOCKS - 1 + 2)

    for k in range(4):
        halo_copy(k).start()
    for i in range(APER):
        following_copy(i).start()
    for k, c in FIRST_SENDS:
        start_window(k, c)

    def square_sums(s, c, first):
        v = ybuf[s, :, c * TILE : (c + 1) * TILE].astype(jnp.float32)
        total = jnp.sum((v * v).reshape(ROWS // 8, 8, TILE), axis=0)
        pow_mine[c] = total if first else pow_mine[c] + total

    def build_lags(s, a):
        keep = jnp.where(jnp.logical_and(s == 0, yl == 0), 0.0, PRESCALE)
        x = ybuf[s, :, a * TILE : (a + 1) * TILE].astype(jnp.float32) * PRESCALE
        h = halo[s, :, a * TILE : (a + 1) * TILE].astype(jnp.float32) * keep
        rows = jnp.concatenate([jnp.zeros((TILE - HALO, TILE), jnp.float32), h, x], axis=0)
        cols = jnp.transpose(rows)
        for j in range(LAGS):
            shifted = cols if j == 0 else pltpu.roll(cols, j, 1)
            amat[s, a, j * TILE : (j + 1) * TILE, :] = shifted[:, TILE:].astype(jnp.bfloat16)

    def products(s, c, first):
        y = ybuf[s, :, c * TILE : (c + 1) * TILE]
        for a in range(2):
            d = c - a
            if 0 <= d < 4:
                p = jnp.dot(amat[s, a], y, preferred_element_type=jnp.float32)
                p = p.reshape(LAGS, TILE, TILE)
                acc[d, a] = p if first else acc[d, a] + p

    def partner_power(c):
        return remote(pow_mine.at[c], pow_other.at[c], p_send.at[c], p_recv.at[c], partner)

    def partner_terms(d, a):
        return remote(send_y.at[d, a], recv_y.at[d, a], y_send.at[d, a], y_recv.at[d, a], partner)

    def compute(c):
        for k in (0, 1, 3, 2):
            s = (z + k) % 4
            if c == 0:
                wait_halo(s)
            if c == 1 and k == 2 and 1 in FORWARDS:
                wait_window(3, 3)
                forward(1).start()
            if not (k == 3 and c == 3 and 1 in FORWARDS):
                wait_window(k, c)
            if k == 1 and c + 2 in FORWARDS:
                forward(c + 2).start()
            if c < 2:
                build_lags(s, c)
            products(s, c, k == 0)
            square_sums(s, c, k == 0)
        if c == 0:
            for i in range(APER):
                following_copy(i).wait_recv()
        for k, e in LATER_SENDS[c]:
            start_window(k, e)
        partner_power(c).start()
        for a in range(2):
            d = c - a
            if 0 <= d < 4:
                for q in range(4):
                    send_y[d, a, q] = acc[d, a, 2 * q + 1 - yl].astype(jnp.bfloat16)
                partner_terms(d, a).start()

    def channel_scale(c):
        total = jnp.sum(pow_mine[c] + pow_other[c], axis=0, keepdims=True)
        return lax.rsqrt(total * (1.0 / (SEGS * ROWS)) + 1e-06)

    def piece_copy(d, k):
        zd = (z + k) % 4
        return remote(
            send_z.at[d, zd], piece[d].at[pl.ds(2 * z, 2)], z_send.at[d, k], z_recv.at[d, z],
            dev(b, 2 * zd + yl),
        )

    def wait_piece(d, k):
        s = (z + k) % 4
        remote(
            send_z.at[d, s], piece[d].at[pl.ds(2 * s, 2)], z_send.at[d, k], z_recv.at[d, s], partner
        ).wait_recv()

    def start_pieces(d):
        if d == 0:
            norm = (1.0 / PRESCALE) * float(SEGS * ROWS) ** -0.5
            for a in range(2):
                partner_power(a).wait_recv()
                row_scale[a] = jnp.transpose(jnp.broadcast_to(channel_scale(a) * norm, (TILE, TILE)))
        else:
            partner_power(d + 1).wait_recv()
        for a in range(2):
            outside = jnp.logical_and(2 * z + d + a >= 8, b == BLOCKS - 1)
            both = row_scale[a] * (channel_scale(d + a) * jnp.where(outside, 0.0, 1.0))
            partner_terms(d, a).wait_recv()
            for q in range(4):
                total = acc[d, a, 2 * q + yl] + recv_y[d, a, q].astype(jnp.float32)
                send_z[d, q, a] = (total * both).astype(jnp.bfloat16)
        for k in (2, 1, 3):
            piece_copy(d, k).start()
        piece[d][pl.ds(2 * z, 2)] = send_z[d, z]

    def owner_copy(d, e):
        o = (b + e) % BLOCKS
        return remote(send_o.at[d, e], recv_o[d].at[b], o_send.at[d, e], o_recv.at[d, b], dev(o, t))

    def wait_owner(d, e):
        s = (b + e) % BLOCKS
        remote(send_o.at[d, e], recv_o[d].at[s], o_send.at[d, e], o_recv.at[d, s], partner).wait_recv()

    def start_owners(d):
        for k in (1, 3, 2):
            wait_piece(d, k)

        def send(e, _):
            send_o[d, e] = piece[d][pos_ref[(b + e) % BLOCKS]]
            owner_copy(d, e).start()
            return 0

        lax.fori_loop(1, BLOCKS, send, 0)
        recv_o[d][b] = piece[d][pos_ref[b]]

    def slot_dst(d, lag):
        return out_ref.at[:, lag, :, pl.ds(d * TILE, TILE)]

    def slot_copy(d, e):
        return remote(
            send_t.at[d, e], slot_dst(d, t), t_send.at[d, e], t_recv.at[d, t],
            dev(b, (t + e) % SEGS),
        )

    def own_slots(d):
        return pltpu.make_async_copy(send_t.at[d, 0], slot_dst(d, t), t_recv.at[d, t])

    def wait_slots(d, e):
        s = (t + e) % SEGS
        remote(send_t.at[d, e], slot_dst(d, s), t_send.at[d, e], t_recv.at[d, s], partner).wait_recv()

    def start_slots(d):
        def arrive(e, _):
            wait_owner(d, e)
            return 0

        lax.fori_loop(1, BLOCKS, arrive, 0)

        def fill(e):
            base = 2 * ((t + e) % SEGS)
            for i in range(2):
                taken = recv_o[d][src_ref[base + i]]
                keep = jnp.broadcast_to(fill_ref[base + i], (TILE, TILE)) > 0
                send_t[d, e, i] = jnp.where(keep, taken.astype(jnp.float32), 0.0).astype(jnp.bfloat16)

        def send(e, _):
            fill(e)
            slot_copy(d, e).start()
            return 0

        lax.fori_loop(1, SEGS, send, 0)
        fill(0)
        own_slots(d).start()

    compute(0)
    compute(1)
    start_pieces(0)
    compute(2)
    start_owners(0)
    start_pieces(1)
    compute(3)
    start_slots(0)
    start_owners(1)
    start_pieces(2)
    compute(4)
    start_slots(1)
    start_owners(2)
    start_pieces(3)
    start_slots(2)
    start_owners(3)
    start_slots(3)

    for k in range(4):
        halo_copy(k).wait_send()
    for i in range(APER):
        following_copy(i).wait_send()
    for c in range(5):
        for k in (1, 2, 3):
            if k == 2 and c in FORWARDS:
                forward(c).wait_send()
            else:
                window_copy(k, c, own_tile(c)).wait_send()
        partner_power(c).wait_send()
    for d in range(4):
        for a in range(2):
            partner_terms(d, a).wait_send()
        for k in (1, 2, 3):
            piece_copy(d, k).wait_send()

        def owner_done(e, _, d=d):
            owner_copy(d, e).wait_send()
            return 0

        lax.fori_loop(1, BLOCKS, owner_done, 0)

        def slot_done(e, _, d=d):
            slot_copy(d, e).wait_send()
            wait_slots(d, e)
            return 0

        lax.fori_loop(1, SEGS, slot_done, 0)
        own_slots(d).wait()


def route(tile_owner):
    owner_table = tile_owner.reshape(BLOCKS, NT_HERE)
    my_index = lax.axis_index(("rowblk", "colblk"))
    my_owners = lax.dynamic_index_in_dim(owner_table, my_index, 0, keepdims=False)
    targets = jnp.arange(BLOCKS, dtype=jnp.int32)
    matches = my_owners[None, :] == targets[:, None]
    local_pos = jnp.sum(
        jnp.where(matches, jnp.arange(NT_HERE, dtype=jnp.int32)[None, :], 0), axis=1
    )
    arrived = jnp.any(owner_table == my_index, axis=1)
    slot_rank = jnp.cumsum(arrived.astype(jnp.int32)) - 1
    picker = (slot_rank[None, :] == jnp.arange(OCAP, dtype=jnp.int32)[:, None]) & arrived[None, :]
    source_of = jnp.sum(jnp.where(picker, targets[None, :], 0), axis=1)
    filled = jnp.any(picker, axis=1).astype(jnp.int32)
    return local_pos, source_of, filled


NT_HERE = 8


def shards(signal, tile_owner):
    local_pos, source_of, filled = route(tile_owner)
    bf16, f32, vmem, dma = jnp.bfloat16, jnp.float32, pltpu.VMEM, pltpu.SemaphoreType.DMA
    out = pl.pallas_call(
        kernel,
        out_shape=jax.ShapeDtypeStruct((2, LAGS, TILE, WIN), bf16),
        in_specs=[pl.BlockSpec(memory_space=pltpu.SMEM)] * 3 + [pl.BlockSpec(memory_space=pl.ANY)],
        out_specs=pl.BlockSpec(memory_space=pl.ANY),
        scratch_shapes=[
            vmem((4, ROWS, 5 * TILE), bf16),
            vmem((4, HALO, HALF), bf16),
            vmem((APER, ROWS, TILE), bf16),
            vmem((4, 2, LAGS * TILE, ROWS), bf16),
            vmem((4, 2, LAGS, TILE, TILE), f32),
            vmem((5, 8, TILE), f32),
            vmem((5, 8, TILE), f32),
            vmem((2, TILE, TILE), f32),
            vmem((4, 2, 4, TILE, TILE), bf16),
            vmem((4, 2, 4, TILE, TILE), bf16),
            vmem((4, 4, 2, TILE, TILE), bf16),
        ]
        + [vmem((8, TILE, TILE), bf16)] * 4
        + [vmem((BLOCKS, TILE, TILE), bf16)] * 4
        + [
            vmem((4, BLOCKS, TILE, TILE), bf16),
            vmem((4, SEGS, 2, TILE, TILE), bf16),
            dma((4, 5)), dma((4, 5)), dma((4,)), dma((3,)), dma((3,)), dma((4,)), dma((4,)), dma((5,)), dma((5,)), dma((4, 2)), dma((4, 2)),
            dma((4, 4)), dma((4, 4)), dma((4, BLOCKS)), dma((4, BLOCKS)), dma((4, SEGS)), dma((4, SEGS)),
        ],
        compiler_params=pltpu.CompilerParams(
            collective_id=0, has_side_effects=True, vmem_limit_bytes=48 * 1024 * 1024
        ),
    )(local_pos, source_of, filled, signal)
    return out.astype(f32)[None]


def solution(mesh):
    return jax.shard_map(
        shards,
        mesh=mesh,
        in_specs=(P("tm", ("rowblk", "colblk")), P()),
        out_specs=P(("rowblk", "colblk"), "tm", None, None, None),
        check_vma=False,
    )
```

time: 222 us -> 128 us (0.58); the launches traced: 220 us -> 128 us
  Pallas kernels: 0 us -> 123 us
  blocking collectives: 118 us -> 0 us
  waiting for transfers between devices: 47.5 us -> 0 us
  starting transfers between devices: 25.8 us -> 0 us
  matrix products: 15.3 us -> 0 us
  other arithmetic: 8.91 us -> 3.2 us
    pallas_call x0 -> x1, Pallas kernels: none -> 123 us  [shards(): pl.pallas_call(kernel, out_shape=jax.ShapeDtypeStruct((2, LAGS, TILE, WIN...]
    all_to_all x2 -> x0, blocking collectives: 100 us -> none  [the longest x1 73 us: shards(): lax.all_to_all(windows, 'tm', split_axis=0, concat_axis=0, tiled=True)]
    all_to_all x2 -> x0, waiting for transfers between devices: 41.1 us -> none  [the longest x1 28.5 us: shards(): lax.all_to_all(outgoing, ('rowblk', 'colblk'), split_axis=0, concat_axis=...]
    psum x1 -> x0, blocking collectives: 18.2 us -> none  [shards(): power_sum = lax.psum(jnp.sum(values * values, axis=0), 'tm')]
    all_to_all x2 -> x0, starting transfers between devices: 17 us -> none  [the longest x1 13.5 us: shards(): lax.all_to_all(outgoing, ('rowblk', 'colblk'), split_axis=0, concat_axis=...]
    dot_general x8 -> x0, matrix products: 15.3 us -> none  [shards(): jnp.einsum('ti,tc->ic', first, later[l:l + total_time], preferred_element...]
    ppermute x1 -> x0, starting transfers between devices: 8.77 us -> none  [passed_along(): return lax.ppermute(block, axis, route)]
    ppermute x1 -> x0, waiting for transfers between devices: 6.41 us -> none  [passed_along(): return lax.ppermute(block, axis, route)]
  transfers between devices with their start and end apart: 3 -> 0, of which waited for: 3 -> 0; matrix products, arithmetic and copies ran while one was open for 1% -> 0% of each run, Pallas kernels for 0% -> 0%
where the time goes in v3:
time: 128 us
  Pallas kernels  123 us (96%)
  other arithmetic  3.2 us (2%)
  local copies, waits for them, and re-layouts  2.23 us (2%)
    pallas_call x1, Pallas kernels, shards(): pl.pallas_call(kernel, out_shape=jax.ShapeDtypeStruct((2, LAGS, TILE, WIN...  123 us
    broadcast_in_dim x1, other arithmetic, shards(): return out.astype(f32)[None]  2.6 us

profile of v3, /device:TPU:1, one launch (start us, length us, event | category | flops | bytes accessed | tf_op | source)
XLA Modules:
  0.0 128.2 jit_solution(5350595839703249431)
XLA Ops:
  0.0 0.7 reshape.36
  0.7 0.1 compare_reduce_fusion
  0.9 0.1 select_reduce_fusion.1.pos_ref
  1.0 0.1 copy.5
  1.1 0.1 add_reduce_fusion
  1.2 0.1 fusion.1
  1.3 0.1 select_reduce_fusion.src_ref
  1.5 0.0 copy-start
  1.5 1.4 %copy-done = bf16[768,1024]{1,0:T(8,128)(2,1)S(1)} copy-done((bf16[768,1024]{1,0:T(8,128)(2,1)S(1)}, bf16[768,1024]{1,0:T(8,128)(2,1)}, u32[]{:S(2)}) %copy-start) | copy-done | bytes 1572888
  2.9 122.7 %shard_map.28 = bf16[2,8,128,512]{3,2,1,0:T(8,128)(2,1)S(1)} custom-call(s32[16]{0:T(128)S(1)} %select_reduce_fusion.1.pos_ref, s32[16]{0:T(128)S(1)} %select_reduce_fusion.src_ref, s32[16]{0:T(128)S(1)} %convert_element_type.21.fill_ref, bf16[768,1024]{1,0:T(8,128)(2,1)S(1)} %copy-done), custom_call_target="tpu_custom_call" | custom-call | tf_op jit(solution)/shard_map/pallas_call | solution.py:362
  125.6 2.6 %bitcast_convert_fusion = f32[1,2,8,128,512]{4,3,2,1,0:T(8,128)} fusion(bf16[2,8,128,512]{3,2,1,0:T(8,128)(2,1)S(1)} %shard_map.28), kind=kLoop, calls=%fused_computation | loop fusion | flops 1048576 | bytes 6291456 | tf_op jit(solution)/shard_map/broadcast_in_dim | solution.py:392
  (4 shorter events, 0.1 us)
Async XLA Ops:
  1.5 1.4 %copy-start = (bf16[768,1024]{1,0:T(8,128)(2,1)S(1)}, bf16[768,1024]{1,0:T(8,128)(2,1)}, u32[]{:S(2)}) copy-start(bf16[768,1024]{1,0:T(8,128)(2,1)} %sig_ref.1) | copy-start | bytes 4718596

commit v4 on v3

--- a/solution.py
+++ b/solution.py
@@ -22,7 +22,7 @@
 FORWARDS = ()
 FIRST_SENDS = ((2, 0), (1, 0), (3, 0), (2, 1), (1, 1), (3, 1))
 LATER_SENDS = (
-    ((2, 2), (1, 2), (3, 2), (0, 2), (2, 3), (1, 3), (3, 3), (0, 3), (2, 4), (1, 4), (3, 4), (0, 4)), (), (), (), (),
+    ((2, 2), (1, 2), (3, 2), (0, 2)), ((2, 3), (1, 3), (3, 3), (0, 3)), ((2, 4), (1, 4), (3, 4), (0, 4)), (), (),
 )
 
 
@@ -152,9 +152,11 @@
         for a in range(2):
             d = c - a
             if 0 <= d < 4:
-                p = jnp.dot(amat[s, a], y, preferred_element_type=jnp.float32)
-                p = p.reshape(LAGS, TILE, TILE)
-                acc[d, a] = p if first else acc[d, a] + p
+                for j in range(0, LAGS, 4):
+                    p = jnp.dot(
+                        amat[s, a, j * TILE : (j + 4) * TILE, :], y, preferred_element_type=jnp.float32
+                    ).reshape(4, TILE, TILE)
+                    acc[d, a, j : j + 4] = p if first else acc[d, a, j : j + 4] + p
 
     def partner_power(c):
         return remote(pow_mine.at[c], pow_other.at[c], p_send.at[c], p_recv.at[c], partner)
@@ -290,18 +292,18 @@
     compute(1)
     start_pieces(0)
     compute(2)
+    start_pieces(1)
     start_owners(0)
-    start_pieces(1)
     compute(3)
+    start_pieces(2)
+    start_owners(1)
+    compute(4)
+    start_pieces(3)
+    start_owners(2)
     start_slots(0)
-    start_owners(1)
-    start_pieces(2)
-    compute(4)
+    start_owners(3)
     start_slots(1)
-    start_owners(2)
-    start_pieces(3)
     start_slots(2)
-    start_owners(3)
     start_slots(3)
 
     for k in range(4):

time: 128 us -> 116 us (0.906)
  Pallas kernels: 123 us -> 111 us
    pallas_call x1, Pallas kernels: 123 us -> 111 us  [shards(): pl.pallas_call(kernel, out_shape=jax.ShapeDtypeStruct((2, LAGS, TILE, WIN...]
where the time goes in v4:
time: 116 us
  Pallas kernels  111 us (96%)
  other arithmetic  3.2 us (3%)
  local copies, waits for them, and re-layouts  2.23 us (2%)
    pallas_call x1, Pallas kernels, shards(): pl.pallas_call(kernel, out_shape=jax.ShapeDtypeStruct((2, LAGS, TILE, WIN...  111 us
    broadcast_in_dim x1, other arithmetic, shards(): return out.astype(f32)[None]  2.6 us

profile of v4, /device:TPU:1, one launch (start us, length us, event | category | flops | bytes accessed | tf_op | source)
XLA Modules:
  0.0 116.3 jit_solution(8975705757137605143)
XLA Ops:
  0.0 0.7 reshape.36
  0.7 0.1 compare_reduce_fusion
  0.9 0.1 select_reduce_fusion.1.pos_ref
  1.0 0.1 copy.5
  1.1 0.1 add_reduce_fusion
  1.2 0.1 fusion.1
  1.3 0.1 select_reduce_fusion.src_ref
  1.5 0.0 copy-start
  1.5 1.4 %copy-done = bf16[768,1024]{1,0:T(8,128)(2,1)S(1)} copy-done((bf16[768,1024]{1,0:T(8,128)(2,1)S(1)}, bf16[768,1024]{1,0:T(8,128)(2,1)}, u32[]{:S(2)}) %copy-start) | copy-done | bytes 1572888
  2.9 110.8 %shard_map.28 = bf16[2,8,128,512]{3,2,1,0:T(8,128)(2,1)S(1)} custom-call(s32[16]{0:T(128)S(1)} %select_reduce_fusion.1.pos_ref, s32[16]{0:T(128)S(1)} %select_reduce_fusion.src_ref, s32[16]{0:T(128)S(1)} %convert_element_type.21.fill_ref, bf16[768,1024]{1,0:T(8,128)(2,1)S(1)} %copy-done), custom_call_target="tpu_custom_call" | custom-call | tf_op jit(solution)/shard_map/pallas_call | solution.py:364
  113.7 2.6 %bitcast_convert_fusion = f32[1,2,8,128,512]{4,3,2,1,0:T(8,128)} fusion(bf16[2,8,128,512]{3,2,1,0:T(8,128)(2,1)S(1)} %shard_map.28), kind=kLoop, calls=%fused_computation | loop fusion | flops 1048576 | bytes 6291456 | tf_op jit(solution)/shard_map/broadcast_in_dim | solution.py:394
  (4 shorter events, 0.1 us)
Async XLA Ops:
  1.5 1.4 %copy-start = (bf16[768,1024]{1,0:T(8,128)(2,1)S(1)}, bf16[768,1024]{1,0:T(8,128)(2,1)}, u32[]{:S(2)}) copy-start(bf16[768,1024]{1,0:T(8,128)(2,1)} %sig_ref.1) | copy-start | bytes 4718596

commit v5 on v4

--- a/solution.py
+++ b/solution.py
@@ -19,7 +19,6 @@
 HALF = 256
 HALO = 16
 PRESCALE = 2.0**40
-FORWARDS = ()
 FIRST_SENDS = ((2, 0), (1, 0), (3, 0), (2, 1), (1, 1), (3, 1))
 LATER_SENDS = (
     ((2, 2), (1, 2), (3, 2), (0, 2)), ((2, 3), (1, 3), (3, 3), (0, 3)), ((2, 4), (1, 4), (3, 4), (0, 4)), (), (),
@@ -30,7 +29,7 @@
     pos_ref, src_ref, fill_ref, sig_ref, out_ref,
     ybuf, halo, following, amat, acc, pow_mine, pow_other, row_scale, send_y, recv_y, send_z,
     piece_0, piece_1, piece_2, piece_3, recv_o_0, recv_o_1, recv_o_2, recv_o_3, send_o, send_t,
-    g_send, g_recv, f_send, n_send, n_recv, h_send, h_recv, p_send, p_recv, y_send, y_recv,
+    g_send, g_recv, n_send, n_recv, h_send, h_recv, p_send, p_recv, y_send, y_recv,
     z_send, z_recv, o_send, o_recv, t_send, t_recv,
 ):
     t = lax.axis_index("tm")
@@ -56,10 +55,6 @@
     barrier = pltpu.get_barrier_semaphore()
     for d in range(1, SEGS):
         pl.semaphore_signal(barrier, inc=1, device_id=dev(b, (t + d) % SEGS), device_id_type=MESH)
-    for d, k in ((1, 2), (BLOCKS - 1, SEGS - 2)):
-        pl.semaphore_signal(
-            barrier, inc=1, device_id=dev((b + d) % BLOCKS, (t + k) % SEGS), device_id_type=MESH
-        )
     for d in range(1, BLOCKS):
         pl.semaphore_signal(barrier, inc=1, device_id=dev((b + d) % BLOCKS, t), device_id_type=MESH)
 
@@ -101,16 +96,6 @@
             own_tile(i), following.at[i], n_send.at[i], n_recv.at[i], dev((b + BLOCKS - 1) % BLOCKS, t)
         )
 
-    def forward(c):
-        step, held = (1, 3) if c == 1 else (3, c - 2)
-        s = (z + 3) % 4 if c == 1 else (z + 1) % 4
-        zd = (z + step) % 4
-        block = (b + (z + step) // 4 + (BLOCKS if c == 1 else BLOCKS - 1)) % BLOCKS
-        return remote(
-            ybuf.at[s, :, pl.ds(held * TILE, TILE)], ybuf.at[s, :, pl.ds(c * TILE, TILE)],
-            f_send.at[c - 1], g_recv.at[s, c], dev(block, 2 * zd + yl),
-        )
-
     def halo_copy(k):
         zd = (z + k) % 4
         slot = (z + yl) % 4
@@ -123,7 +108,7 @@
     for c in range(2):
         start_window(0, c)
 
-    pl.semaphore_wait(barrier, SEGS - 1 + BLOCKS - 1 + 2)
+    pl.semaphore_wait(barrier, SEGS - 1 + BLOCKS - 1)
 
     for k in range(4):
         halo_copy(k).start()
@@ -169,13 +154,7 @@
             s = (z + k) % 4
             if c == 0:
                 wait_halo(s)
-            if c == 1 and k == 2 and 1 in FORWARDS:
-                wait_window(3, 3)
-                forward(1).start()
-            if not (k == 3 and c == 3 and 1 in FORWARDS):
-                wait_window(k, c)
-            if k == 1 and c + 2 in FORWARDS:
-                forward(c + 2).start()
+            wait_window(k, c)
             if c < 2:
                 build_lags(s, c)
             products(s, c, k == 0)
@@ -241,7 +220,8 @@
         for k in (1, 3, 2):
             wait_piece(d, k)
 
-        def send(e, _):
+        def send(i, _):
+            e = (i * 7) % BLOCKS
             send_o[d, e] = piece[d][pos_ref[(b + e) % BLOCKS]]
             owner_copy(d, e).start()
             return 0
@@ -292,17 +272,17 @@
     compute(1)
     start_pieces(0)
     compute(2)
+    start_owners(0)
     start_pieces(1)
-    start_owners(0)
     compute(3)
+    start_owners(1)
     start_pieces(2)
-    start_owners(1)
+    start_slots(0)
     compute(4)
+    start_owners(2)
     start_pieces(3)
-    start_owners(2)
-    start_slots(0)
+    start_slots(1)
     start_owners(3)
-    start_slots(1)
     start_slots(2)
     start_slots(3)
 
@@ -312,10 +292,7 @@
         following_copy(i).wait_send()
     for c in range(5):
         for k in (1, 2, 3):
-            if k == 2 and c in FORWARDS:
-                forward(c).wait_send()
-            else:
-                window_copy(k, c, own_tile(c)).wait_send()
+            window_copy(k, c, own_tile(c)).wait_send()
         partner_power(c).wait_send()
     for d in range(4):
         for a in range(2):
@@ -384,7 +361,7 @@
         + [
             vmem((4, BLOCKS, TILE, TILE), bf16),
             vmem((4, SEGS, 2, TILE, TILE), bf16),
-            dma((4, 5)), dma((4, 5)), dma((4,)), dma((3,)), dma((3,)), dma((4,)), dma((4,)), dma((5,)), dma((5,)), dma((4, 2)), dma((4, 2)),
+            dma((4, 5)), dma((4, 5)), dma((3,)), dma((3,)), dma((4,)), dma((4,)), dma((5,)), dma((5,)), dma((4, 2)), dma((4, 2)),
             dma((4, 4)), dma((4, 4)), dma((4, BLOCKS)), dma((4, BLOCKS)), dma((4, SEGS)), dma((4, SEGS)),
         ],
         compiler_params=pltpu.CompilerParams(

time: 116 us -> 114 us (0.983)
  Pallas kernels: 111 us -> 108 us
    pallas_call x1, Pallas kernels: 111 us -> 108 us  [shards(): pl.pallas_call(kernel, out_shape=jax.ShapeDtypeStruct((2, LAGS, TILE, WIN...]
where the time goes in v5:
time: 114 us; the launch traced here: 113 us
  Pallas kernels  108 us (95%)
  other arithmetic  3.2 us (3%)
  local copies, waits for them, and re-layouts  2.23 us (2%)
    pallas_call x1, Pallas kernels, shards(): pl.pallas_call(kernel, out_shape=jax.ShapeDtypeStruct((2, LAGS, TILE, WIN...  108 us
    broadcast_in_dim x1, other arithmetic, shards(): return out.astype(f32)[None]  2.6 us

profile of v5, /device:TPU:1, one launch (start us, length us, event | category | flops | bytes accessed | tf_op | source)
XLA Modules:
  0.0 113.2 jit_solution(2054289935037549076)
XLA Ops:
  0.0 0.7 reshape.36
  0.7 0.1 compare_reduce_fusion
  0.9 0.1 select_reduce_fusion.1.pos_ref
  1.0 0.1 copy.5
  1.1 0.1 add_reduce_fusion
  1.2 0.1 fusion.1
  1.3 0.1 select_reduce_fusion.src_ref
  1.5 0.0 copy-start
  1.5 1.4 %copy-done = bf16[768,1024]{1,0:T(8,128)(2,1)S(1)} copy-done((bf16[768,1024]{1,0:T(8,128)(2,1)S(1)}, bf16[768,1024]{1,0:T(8,128)(2,1)}, u32[]{:S(2)}) %copy-start) | copy-done | bytes 1572888
  2.9 107.7 %shard_map.28 = bf16[2,8,128,512]{3,2,1,0:T(8,128)(2,1)S(1)} custom-call(s32[16]{0:T(128)S(1)} %select_reduce_fusion.1.pos_ref, s32[16]{0:T(128)S(1)} %select_reduce_fusion.src_ref, s32[16]{0:T(128)S(1)} %convert_element_type.21.fill_ref, bf16[768,1024]{1,0:T(8,128)(2,1)S(1)} %copy-done), custom_call_target="tpu_custom_call" | custom-call | tf_op jit(solution)/shard_map/pallas_call | solution.py:341
  110.6 2.6 %bitcast_convert_fusion = f32[1,2,8,128,512]{4,3,2,1,0:T(8,128)} fusion(bf16[2,8,128,512]{3,2,1,0:T(8,128)(2,1)S(1)} %shard_map.28), kind=kLoop, calls=%fused_computation | loop fusion | flops 1048576 | bytes 6291456 | tf_op jit(solution)/shard_map/broadcast_in_dim | solution.py:371
  (4 shorter events, 0.1 us)
Async XLA Ops:
  1.5 1.4 %copy-start = (bf16[768,1024]{1,0:T(8,128)(2,1)S(1)}, bf16[768,1024]{1,0:T(8,128)(2,1)}, u32[]{:S(2)}) copy-start(bf16[768,1024]{1,0:T(8,128)(2,1)} %sig_ref.1) | copy-start | bytes 4718596

commit v6 on v5

--- a/solution.py
+++ b/solution.py
@@ -221,7 +221,7 @@
             wait_piece(d, k)
 
         def send(i, _):
-            e = (i * 7) % BLOCKS
+            e = (i * 3) % BLOCKS
             send_o[d, e] = piece[d][pos_ref[(b + e) % BLOCKS]]
             owner_copy(d, e).start()
             return 0
@@ -277,8 +277,8 @@
     compute(3)
     start_owners(1)
     start_pieces(2)
+    compute(4)
     start_slots(0)
-    compute(4)
     start_owners(2)
     start_pieces(3)
     start_slots(1)

time: 114 us -> 113 us (level)
  no operation moved by 1% of the time
where the time goes in v6:
time: 113 us
  Pallas kernels  108 us (96%)
  other arithmetic  3.2 us (3%)
  local copies, waits for them, and re-layouts  2.23 us (2%)
    pallas_call x1, Pallas kernels, shards(): pl.pallas_call(kernel, out_shape=jax.ShapeDtypeStruct((2, LAGS, TILE, WIN...  108 us
    broadcast_in_dim x1, other arithmetic, shards(): return out.astype(f32)[None]  2.6 us

profile of v6, /device:TPU:1, one launch (start us, length us, event | category | flops | bytes accessed | tf_op | source)
XLA Modules:
  0.0 113.0 jit_solution(3752064122596540636)
XLA Ops:
  0.0 0.7 reshape.36
  0.7 0.1 compare_reduce_fusion
  0.9 0.1 select_reduce_fusion.1.pos_ref
  1.0 0.1 copy.5
  1.1 0.1 add_reduce_fusion
  1.2 0.1 fusion.1
  1.3 0.1 select_reduce_fusion.src_ref
  1.5 0.0 copy-start
  1.5 1.4 %copy-done = bf16[768,1024]{1,0:T(8,128)(2,1)S(1)} copy-done((bf16[768,1024]{1,0:T(8,128)(2,1)S(1)}, bf16[768,1024]{1,0:T(8,128)(2,1)}, u32[]{:S(2)}) %copy-start) | copy-done | bytes 1572888
  2.9 107.5 %shard_map.28 = bf16[2,8,128,512]{3,2,1,0:T(8,128)(2,1)S(1)} custom-call(s32[16]{0:T(128)S(1)} %select_reduce_fusion.1.pos_ref, s32[16]{0:T(128)S(1)} %select_reduce_fusion.src_ref, s32[16]{0:T(128)S(1)} %convert_element_type.21.fill_ref, bf16[768,1024]{1,0:T(8,128)(2,1)S(1)} %copy-done), custom_call_target="tpu_custom_call" | custom-call | tf_op jit(solution)/shard_map/pallas_call | solution.py:341
  110.4 2.6 %bitcast_convert_fusion = f32[1,2,8,128,512]{4,3,2,1,0:T(8,128)} fusion(bf16[2,8,128,512]{3,2,1,0:T(8,128)(2,1)S(1)} %shard_map.28), kind=kLoop, calls=%fused_computation | loop fusion | flops 1048576 | bytes 6291456 | tf_op jit(solution)/shard_map/broadcast_in_dim | solution.py:371
  (4 shorter events, 0.1 us)
Async XLA Ops:
  1.5 1.4 %copy-start = (bf16[768,1024]{1,0:T(8,128)(2,1)S(1)}, bf16[768,1024]{1,0:T(8,128)(2,1)}, u32[]{:S(2)}) copy-start(bf16[768,1024]{1,0:T(8,128)(2,1)} %sig_ref.1) | copy-start | bytes 4718596

commit v7 on v6

--- a/solution.py
+++ b/solution.py
@@ -278,11 +278,11 @@
     start_owners(1)
     start_pieces(2)
     compute(4)
+    start_owners(2)
     start_slots(0)
-    start_owners(2)
     start_pieces(3)
+    start_owners(3)
     start_slots(1)
-    start_owners(3)
     start_slots(2)
     start_slots(3)
 

time: 113 us -> 114 us (level)
  no operation moved by 1% of the time
where the time goes in v7:
time: 114 us; the launch traced here: 113 us
  Pallas kernels  108 us (95%)
  other arithmetic  3.2 us (3%)
  local copies, waits for them, and re-layouts  2.23 us (2%)
    pallas_call x1, Pallas kernels, shards(): pl.pallas_call(kernel, out_shape=jax.ShapeDtypeStruct((2, LAGS, TILE, WIN...  108 us
    broadcast_in_dim x1, other arithmetic, shards(): return out.astype(f32)[None]  2.6 us

profile of v7, /device:TPU:1, one launch (start us, length us, event | category | flops | bytes accessed | tf_op | source)
XLA Modules:
  0.0 113.2 jit_solution(7201123961358939133)
XLA Ops:
  0.0 0.7 reshape.36
  0.7 0.1 compare_reduce_fusion
  0.9 0.1 select_reduce_fusion.1.pos_ref
  1.0 0.1 copy.5
  1.1 0.1 add_reduce_fusion
  1.2 0.1 fusion.1
  1.3 0.1 select_reduce_fusion.src_ref
  1.5 0.0 copy-start
  1.5 1.4 %copy-done = bf16[768,1024]{1,0:T(8,128)(2,1)S(1)} copy-done((bf16[768,1024]{1,0:T(8,128)(2,1)S(1)}, bf16[768,1024]{1,0:T(8,128)(2,1)}, u32[]{:S(2)}) %copy-start) | copy-done | bytes 1572888
  2.9 107.7 %shard_map.28 = bf16[2,8,128,512]{3,2,1,0:T(8,128)(2,1)S(1)} custom-call(s32[16]{0:T(128)S(1)} %select_reduce_fusion.1.pos_ref, s32[16]{0:T(128)S(1)} %select_reduce_fusion.src_ref, s32[16]{0:T(128)S(1)} %convert_element_type.21.fill_ref, bf16[768,1024]{1,0:T(8,128)(2,1)S(1)} %copy-done), custom_call_target="tpu_custom_call" | custom-call | tf_op jit(solution)/shard_map/pallas_call | solution.py:341
  110.6 2.6 %bitcast_convert_fusion = f32[1,2,8,128,512]{4,3,2,1,0:T(8,128)} fusion(bf16[2,8,128,512]{3,2,1,0:T(8,128)(2,1)S(1)} %shard_map.28), kind=kLoop, calls=%fused_computation | loop fusion | flops 1048576 | bytes 6291456 | tf_op jit(solution)/shard_map/broadcast_in_dim | solution.py:371
  (4 shorter events, 0.1 us)
Async XLA Ops:
  1.5 1.4 %copy-start = (bf16[768,1024]{1,0:T(8,128)(2,1)S(1)}, bf16[768,1024]{1,0:T(8,128)(2,1)}, u32[]{:S(2)}) copy-start(bf16[768,1024]{1,0:T(8,128)(2,1)} %sig_ref.1) | copy-start | bytes 4718596
